TPU v7x, 256 devices: a whole 4x4x8 slice. The times are simulated.
256 devices in a mesh: patch: 64 (over z, y, core), sample: 4 (over x).
Axes of the slice: x: 4, y: 4, z: 8, core: 2. Of those that a mesh axis runs over, the one named last changes fastest.
Arguments:
- features: bfloat16 [4, 32768, 512], P('sample', 'patch'), may hold values from -600 to 600
- cotangent: bfloat16 [4, 32768, 512], P('sample', 'patch'), may hold values from -6 to 6
- weight_qkv: bfloat16 [512, 1536], replicated, may hold values from -5 to 5
- weight_out: bfloat16 [512, 512], replicated, may hold values from -0.25 to 0.25
- key_tiles: int32 [256, 8], replicated, may hold values from 0 to 255, as said below
- tile_valid: int32 [256, 8], replicated, may hold values from 0 to 1, as said below
Outputs:
- grad_features: bfloat16 [4, 32768, 512], P('sample', 'patch')
- grad_qkv: float32 [512, 1536], replicated
- grad_out: float32 [512, 512], replicated
Inputs may be any that keep to these rules, and one draw needn't show every extreme that they name: `key_tiles`: row g names 8 distinct tile ids. A tile's patch is its id // 4. The first id is g itself, the next 3 are other tiles of g's patch, and the last 4 lie one each in the patches at offsets -2 to 2 other than 0 around the cycle of patches, in rising order of offset. Over the rows of one patch exactly 2 distinct tiles of each such neighbouring patch are named. `tile_valid`: column 0 is always 1.
All inputs are finite; a program needn't handle non-finite values.
Results may differ from a plain program's by a relative error of at most 0.0088.
Values may be sent and summed in bfloat16 or wider, within the bound.
A program may use at most 192 MiB of HBM per device.

v0:
```python
from functools import partial
import math
import jax
import jax.numpy as jnp
from jax import lax
from jax.sharding import PartitionSpec as P

HEADS = 4
TILE = 128
NB = 8
REACH = 2
epsilon = 1e-06


def from_behind(value, axis, steps):
    count = lax.axis_size(axis)
    pairs = [(source, (source + steps) % count) for source in range(count)]
    return lax.ppermute(value, axis, pairs)


def tile_backward(query_tile, pair_tiles, live_flags, grad_tile, head_count):
    row_count = query_tile.shape[0]
    model_width = query_tile.shape[1]
    head_width = model_width // head_count
    scaling = head_width ** (-0.5)
    key_heads = pair_tiles[:, :, :model_width].reshape(-1, head_count, head_width)
    value_heads = pair_tiles[:, :, model_width:].reshape(-1, head_count, head_width)
    query_heads = query_tile.reshape(row_count, head_count, head_width)
    grad_heads = grad_tile.reshape(row_count, head_count, head_width)
    scores = (
        jnp.einsum("qhd,khd->hqk", query_heads, key_heads, preferred_element_type=jnp.float32)
        * scaling
    )
    live_mask = jnp.repeat(live_flags > 0, pair_tiles.shape[1])
    scores = jnp.where(live_mask[None, None, :], scores, -jnp.inf)
    highest = jnp.max(scores, -1, keepdims=True)
    expanded = jnp.exp(scores - highest)
    attention = expanded / jnp.sum(expanded, -1, keepdims=True)
    attention_low = attention.astype(jnp.bfloat16)
    attended = jnp.einsum(
        "hqk,khd->qhd", attention_low, value_heads, preferred_element_type=jnp.float32
    )
    attended = attended.astype(jnp.bfloat16).reshape(row_count, model_width)
    dprob = jnp.einsum("qhd,khd->hqk", grad_heads, value_heads, preferred_element_type=jnp.float32)
    centre = jnp.sum(attention * dprob, -1, keepdims=True)
    dscore = (attention * (dprob - centre) * scaling).astype(jnp.bfloat16)
    dquery = jnp.einsum(
        "hqk,khd->qhd", dscore, key_heads, preferred_element_type=jnp.float32
    ).reshape(row_count, model_width)
    dkey = jnp.einsum("hqk,qhd->khd", dscore, query_heads, preferred_element_type=jnp.float32)
    dvalue = jnp.einsum(
        "hqk,qhd->khd", attention_low, grad_heads, preferred_element_type=jnp.float32
    )
    dkey = dkey.reshape(pair_tiles.shape[0], pair_tiles.shape[1], model_width)
    dvalue = dvalue.reshape(pair_tiles.shape[0], pair_tiles.shape[1], model_width)
    return (attended, dquery, jnp.concatenate([dkey, dvalue], -1))


def on_device(features, cotangent, weight_qkv, weight_out, key_tiles, tile_valid):
    patches = lax.axis_size("patch")
    position = lax.axis_index("patch")
    rows_local = features.shape[1]
    model_width = features.shape[2]
    tile_count = rows_local // TILE
    offsets = [shift_by for shift_by in range(-REACH, REACH + 1) if shift_by != 0]
    inputs = features[0].astype(jnp.float32)
    inverse = lax.rsqrt(jnp.mean(inputs * inputs, -1, keepdims=True) + epsilon)
    normed = inputs * inverse
    normed_low = normed.astype(jnp.bfloat16)
    projected = jnp.dot(normed_low, weight_qkv, preferred_element_type=jnp.float32).astype(
        jnp.bfloat16
    )
    queries = projected[:, :model_width]
    pairs_own = projected[:, model_width:].reshape(tile_count, TILE, 2 * model_width)
    grad_rows = cotangent[0]
    grad_attended = jnp.einsum(
        "pe,de->pd", grad_rows, weight_out, preferred_element_type=jnp.float32
    ).astype(jnp.bfloat16)
    my_lists = lax.dynamic_slice_in_dim(key_tiles, position * tile_count, tile_count, 0)
    my_valid = lax.dynamic_slice_in_dim(tile_valid, position * tile_count, tile_count, 0)
    owner_patch = my_lists // tile_count
    within = my_lists % tile_count
    distance = (owner_patch - position) % patches
    distance = jnp.where(distance > patches // 2, distance - patches, distance)
    order_index = jnp.where(distance < 0, distance + REACH, distance + REACH - 1)
    arrivals = []
    for shift_by in offsets:
        arrivals.append(from_behind(pairs_own, "patch", -shift_by))
    buffer = jnp.concatenate([pairs_own] + arrivals, 0)
    slot_ids = jnp.where(distance == 0, within, tile_count + order_index * tile_count + within)
    group_size = math.gcd(4, tile_count)
    step_count = tile_count // group_size
    tile_pass = jax.vmap(partial(tile_backward, head_count=HEADS))
    buffer_count = buffer.shape[0]

    def advance(running, pieces):
        query_group, slot_group, live_group, grad_group = pieces
        flat_slots = slot_group.reshape(-1)
        gathered = jnp.take(buffer, flat_slots, axis=0).reshape(
            group_size, NB, TILE, 2 * model_width
        )
        attended, dquery, dpairs = tile_pass(query_group, gathered, live_group, grad_group)
        running = running.at[flat_slots].add(dpairs.reshape(group_size * NB, TILE, 2 * model_width))
        return (running, (attended, dquery))

    start_sums = jnp.zeros((buffer_count, TILE, 2 * model_width), jnp.float32)
    scanned = (
        queries.reshape(step_count, group_size, TILE, model_width),
        slot_ids.reshape(step_count, group_size, NB),
        my_valid.reshape(step_count, group_size, NB),
        grad_attended.reshape(step_count, group_size, TILE, model_width),
    )
    totals, (attended_all, dquery_all) = lax.scan(advance, start_sums, scanned)
    grads_own = totals[:tile_count]
    for offset_index, shift_by in enumerate(offsets):
        portion = totals[
            tile_count + offset_index * tile_count : tile_count + (offset_index + 1) * tile_count
        ]
        grads_own = grads_own + from_behind(portion.astype(jnp.bfloat16), "patch", shift_by).astype(
            portion.dtype
        )
    attended_rows = attended_all.reshape(rows_local, model_width)
    grad_projected = jnp.concatenate(
        [
            dquery_all.reshape(rows_local, model_width),
            grads_own.reshape(rows_local, 2 * model_width),
        ],
        1,
    ).astype(jnp.bfloat16)
    grad_normed = jnp.einsum(
        "pe,de->pd", grad_projected, weight_qkv, preferred_element_type=jnp.float32
    )
    grad_inputs = grad_rows.astype(jnp.float32) + inverse * (
        grad_normed - normed * jnp.mean(grad_normed * normed, -1, keepdims=True)
    )
    local_qkv = jnp.einsum(
        "pd,pe->de", normed_low, grad_projected, preferred_element_type=jnp.float32
    )
    local_out = jnp.einsum(
        "pd,pe->de", attended_rows, grad_rows, preferred_element_type=jnp.float32
    )
    summed_qkv, summed_out = lax.psum((local_qkv, local_out), ("patch", "sample"))
    factor = float(lax.axis_size("patch") * lax.axis_size("sample") * rows_local) ** (-0.5)
    return (grad_inputs.astype(jnp.bfloat16)[None], summed_qkv * factor, summed_out * factor)


def solution(mesh):
    placed = (P("sample", "patch", None), P("sample", "patch", None), P(), P(), P(), P())
    return jax.shard_map(
        on_device,
        mesh=mesh,
        in_specs=placed,
        out_specs=(P("sample", "patch", None), P(), P()),
        check_vma=False,
    )
```

profile of v0, /device:TPU:2, one launch (start us, length us, event | category | flops | bytes accessed | tf_op | source)
XLA Modules:
  0.0 587.7 jit_solution(10732911310257279190)
XLA Ops:
  13.6 6.2 %collective-permute-start.2 = (bf16[4,128,1024]{2,1,0:T(8,128)(2,1)}, bf16[4,128,1024]{2,1,0:T(8,128)(2,1)}, u32[]{:S(2)}, u32[]{:S(2)}) collective-permute-start(bf16[4,128,1024]{2,1,0:T(8,128)(2,1)} %bitcast.3), channel_id=1, source_target_pairs={{0,252},{4,0},{8,4},{12,8},{16,12},{20,16},{24,20},{28,24},{32,28}... | collective-permute-start | bytes 3145736 | tf_op jit(solution)/shard_map/ppermute | solution.py:18
  19.8 2.3 collective-permute-start.3
  32.8 11.9 %collective-permute-done = bf16[4,128,1024]{2,1,0:T(8,128)(2,1)} collective-permute-done((bf16[4,128,1024]{2,1,0:T(8,128)(2,1)}, bf16[4,128,1024]{2,1,0:T(8,128)(2,1)}, u32[]{:S(2)}, u32[]{:S(2)}) %collective-permute-start) | collective-permute-done | bytes 1048608 | tf_op jit(solution)/shard_map/ppermute | solution.py:18
  44.7 2.3 constant_dynamic-update-slice_fusion.3
  47.0 8.1 %collective-permute-done.1 = bf16[4,128,1024]{2,1,0:T(8,128)(2,1)} collective-permute-done((bf16[4,128,1024]{2,1,0:T(8,128)(2,1)}, bf16[4,128,1024]{2,1,0:T(8,128)(2,1)}, u32[]{:S(2)}, u32[]{:S(2)}) %collective-permute-start.1) | collective-permute-done | bytes 1048608 | tf_op jit(solution)/shard_map/ppermute | solution.py:18
  61.9 7.6 %gather_fusion = bf16[32,128,1024]{2,1,0:T(8,128)(2,1)} fusion(bf16[20,128,1024]{2,1,0:T(8,128)(2,1)} %constant_dynamic-update-slice_fusion, s32[1024]{0:T(1024)S(1)} %pad_clamp_fusion), kind=kCustom, calls=%fused_computation | custom fusion | bytes 16777344 | tf_op jit(solution)/shard_map/while/body/eval_jaxpr/jit(_take)/gather | solution.py:99
  69.5 7.5 %broadcast_select_fusion = bf16[4,8,128,1024]{3,2,1,0:T(8,128)(2,1)} fusion(bf16[4,8,128,1024]{3,2,1,0:T(8,128)(2,1)} %bitcast.63, pred[4,8]{1,0:T(4,128)(4,1)S(1)} %copy.39), kind=kLoop, calls=%fused_computation.10 | loop fusion | flops 4194304 | bytes 16777248 | tf_op jit(solution)/shard_map/while/body/eval_jaxpr/jit(_take)/select_n | solution.py:99
  77.0 5.9 fusion.70
  82.9 6.9 %reshape.155 = bf16[4,1024,4,128]{3,2,1,0:T(4,128)(2,1)} reshape(bf16[4,8,128,512]{3,2,1,0:T(8,128)(2,1)} %get-tuple-element.44) | data formatting | bytes 8388608 | tf_op jit(solution)/shard_map/while/body/eval_jaxpr/vmap()/reshape | solution.py:26
  89.8 7.6 %copy.57 = bf16[4,1024,4,128]{1,3,2,0:T(8,128)(2,1)} copy(bf16[4,1024,4,128]{3,2,1,0:T(4,128)(2,1)} %reshape.155) | data formatting | bytes 8388608 | tf_op jit(solution)/shard_map/while/body/eval_jaxpr/vmap()/reshape | solution.py:26
  97.3 6.9 %reshape.156 = bf16[4,1024,4,128]{3,2,1,0:T(4,128)(2,1)} reshape(bf16[4,8,128,512]{3,2,1,0:T(8,128)(2,1)} %get-tuple-element.43) | data formatting | bytes 8388608 | tf_op jit(solution)/shard_map/while/body/eval_jaxpr/vmap()/reshape | solution.py:27
  104.2 7.5 %copy.56 = bf16[4,1024,4,128]{1,3,2,0:T(8,128)(2,1)} copy(bf16[4,1024,4,128]{3,2,1,0:T(4,128)(2,1)} %reshape.156) | data formatting | bytes 8388608 | tf_op jit(solution)/shard_map/while/body/eval_jaxpr/vmap()/reshape | solution.py:27
  111.7 6.7 %fusion.73 = f32[4,4,128,1024]{3,2,1,0:T(8,128)} fusion(bf16[4,128,4,128]{1,3,2,0:T(8,128)(2,1)S(1)} %copy.51, bf16[4,1024,4,128]{1,3,2,0:T(8,128)(2,1)} %copy.56), kind=kOutput, calls=%fused_computation.98 | convolution fusion | flops 536870912 | bytes 13107200 | tf_op jit(solution)/shard_map/while/body/eval_jaxpr/vmap(qhd,khd->hqk)/dot_general | solution.py:44
  118.4 8.8 %fusion.72 = (f32[4,4,128]{2,1,0:T(4,128)S(1)}, f32[4,4,128,1024]{3,2,1,0:T(8,128)}) fusion(pred[4,1024]{1,0:T(4,128)(4,1)S(1)} %bitcast.70, bf16[4,128,4,128]{1,3,2,0:T(8,128)(2,1)} %copy.49, bf16[4,1024,4,128]{1,3,2,0:T(8,128)(2,1)} %copy.57), kind=kOutput, calls=%fused_computation.97 | convolution fusion | flops 545260544 | bytes 13119488 | tf_op jit(solution)/shard_map/while/body/eval_jaxpr/vmap()/sub | solution.py:37
  127.2 7.9 %convolution_bitcast_fusion = f32[4,1024,4,128]{1,3,2,0:T(8,128)} fusion(bf16[4,128,4,128]{1,3,2,0:T(8,128)(2,1)S(1)} %copy.51, f32[4,4,128,1024]{3,2,1,0:T(8,128)} %get-tuple-element.50, f32[4,4,128]{2,1,0:T(4,128)S(1)} %get-tuple-element.49), kind=kOutput, calls=%fused_computation.19 | convolution fusion | flops 541065216 | bytes 17309696 | tf_op jit(solution)/shard_map/while/body/eval_jaxpr/vmap(hqk,qhd->khd)/dot_general | solution.py:51
  135.1 24.0 %fusion.15 = f32[4,1024,4,128]{1,3,2,0:T(8,128)} fusion(bf16[4,128,4,128]{1,3,2,0:T(8,128)(2,1)} %copy.49, f32[4,4,128,1024]{3,2,1,0:T(8,128)} %fusion.73, f32[4,4,128,1024]{3,2,1,0:T(8,128)} %get-tuple-element.50, f32[4,4,128]{2,1,0:T(4,128)S(1)} %get-tuple-element.49), kind=kOutput, calls=%fused_computation.18 | convolution fusion | flops 551554048 | bytes 25698304 | tf_op jit(solution)/shard_map/while/body/eval_jaxpr/vmap(hqk,qhd->khd)/dot_general | solution.py:50
  159.1 9.9 %copy.50 = f32[4,1024,4,128]{3,2,1,0:T(4,128)} copy(f32[4,1024,4,128]{1,3,2,0:T(8,128)} %fusion.15) | data formatting | bytes 16777216 | tf_op jit(solution)/shard_map/while/body/eval_jaxpr/vmap(hqk,qhd->khd)/transpose | solution.py:50
  169.0 10.3 %concatenate.17 = f32[32,128,512]{2,1,0:T(8,128)} reshape(f32[4,1024,4,128]{3,2,1,0:T(4,128)} %copy.50) | data formatting | bytes 16777216 | tf_op jit(solution)/shard_map/while/body/eval_jaxpr/vmap()/concatenate | solution.py:56
  179.3 9.9 %copy.52 = f32[4,1024,4,128]{3,2,1,0:T(4,128)} copy(f32[4,1024,4,128]{1,3,2,0:T(8,128)} %convolution_bitcast_fusion) | data formatting | bytes 16777216 | tf_op jit(solution)/shard_map/while/body/eval_jaxpr/vmap(hqk,qhd->khd)/transpose | solution.py:51
  189.1 10.3 %concatenate.18 = f32[32,128,512]{2,1,0:T(8,128)} reshape(f32[4,1024,4,128]{3,2,1,0:T(4,128)} %copy.52) | data formatting | bytes 16777216 | tf_op jit(solution)/shard_map/while/body/eval_jaxpr/vmap()/concatenate | solution.py:56
  199.4 11.7 %pad_maximum_fusion = f32[32,128,1024]{2,1,0:T(8,128)} fusion(f32[32,128,512]{2,1,0:T(8,128)} %concatenate.18, f32[32,128,512]{2,1,0:T(8,128)} %concatenate.17), kind=kLoop, calls=%fused_computation.4 | loop fusion | flops 4194304 | bytes 33554432 | tf_op jit(solution)/shard_map/while/body/eval_jaxpr/vmap()/concatenate | solution.py:56
  211.1 5.2 broadcast_in_dim.64
  216.3 36.2 %scatter_fusion = f32[20,128,1024]{2,1,0:T(8,128)} fusion(f32[20,128,1024]{2,1,0:T(8,128)} %broadcast_in_dim.64, s32[32]{0:T(128)S(1)} %fusion.61, f32[32,128,1024]{2,1,0:T(8,128)} %pad_maximum_fusion), kind=kCustom, calls=%fused_computation.1 | custom fusion | flops 4194304 | bytes 50331776 | tf_op jit(solution)/shard_map/while/body/eval_jaxpr/scatter-add | solution.py:103
  252.5 4.8 convert.17
  257.3 2.3 fusion.71
  262.2 4.7 fusion.34
  268.0 22.9 %fusion.37 = bf16[4,128,4,128]{1,3,2,0:T(8,128)(2,1)S(1)} fusion(bf16[4,1024,4,128]{1,3,2,0:T(8,128)(2,1)} %copy.57, f32[4,4,128,1024]{3,2,1,0:T(8,128)} %fusion.73, f32[4,4,128,1024]{3,2,1,0:T(8,128)} %get-tuple-element.50, f32[4,4,128]{2,1,0:T(4,128)S(1)} %get-tuple-element.49), kind=kOutput, calls=%fused_computation.40 | convolution fusion | flops 551816192 | bytes 21504000 | tf_op jit(solution)/shard_map/while/body/eval_jaxpr/vmap(hqk,khd->qhd)/dot_general | solution.py:47
  293.1 2.5 fusion.49
  295.6 3.8 fusion.21
  300.4 2.6 fusion.46
  307.7 268.1 %all-reduce.3.cloned.1.call-done = (f32[512,1536]{1,0:T(8,128)}, f32[512,512]{1,0:T(8,128)}) async-done(((f32[512,1536]{1,0:T(8,128)}, f32[512,512]{1,0:T(8,128)}), (f32[512,1536]{1,0:T(8,128)}, f32[512,512]{1,0:T(8,128)})) %all-reduce.3.cloned.1.call-update) | async-done | bytes 4194320 | tf_op jit(solution)/shard_map/psum | solution.py:142
  575.8 4.0 broadcast_multiply_fusion
  (65 shorter events, 36.3 us)
Async XLA Ops:
  7.2 1.6 copy-start
  7.2 15.0 %copy-start.7 = (s32[256,8]{0,1:T(8,128)S(1)}, s32[256,8]{0,1:T(8,128)}, u32[]{:S(2)}) copy-start(s32[256,8]{0,1:T(8,128)} %param.10) | copy-start | bytes 24580
  7.2 15.0 %copy-start.8 = (s32[256,8]{0,1:T(8,128)S(1)}, s32[256,8]{0,1:T(8,128)}, u32[]{:S(2)}) copy-start(s32[256,8]{0,1:T(8,128)} %param.11) | copy-start | bytes 24580
  7.2 568.6 %all-reduce.3.cloned.1.call-start = ((), (), s32[]{:S(2)}) async-start(), calls=%async_computation | async-start | bytes 8388608 | tf_op jit(solution)/shard_map/psum | solution.py:142
  8.8 18.0 %copy-start.2 = (bf16[1,512,512]{2,1,0:T(8,128)(2,1)S(1)}, bf16[1,512,512]{2,1,0:T(8,128)(2,1)}, u32[]{:S(2)}) copy-start(bf16[1,512,512]{2,1,0:T(8,128)(2,1)} %param.7) | copy-start | bytes 1572868
  9.8 1.1 copy-start.5
  12.1 32.6 %collective-permute-start = (bf16[4,128,1024]{2,1,0:T(8,128)(2,1)}, bf16[4,128,1024]{2,1,0:T(8,128)(2,1)}, u32[]{:S(2)}, u32[]{:S(2)}) collective-permute-start(bf16[4,128,1024]{2,1,0:T(8,128)(2,1)} %bitcast.3), channel_id=1, source_target_pairs={{0,8},{4,12},{8,16},{12,20},{16,24},{20,28},{24,32},{28,36},{32,40... | collective-permute-start | bytes 3145736 | tf_op jit(solution)/shard_map/ppermute | solution.py:18
  13.6 41.4 %collective-permute-start.1 = (bf16[4,128,1024]{2,1,0:T(8,128)(2,1)}, bf16[4,128,1024]{2,1,0:T(8,128)(2,1)}, u32[]{:S(2)}, u32[]{:S(2)}) collective-permute-start(bf16[4,128,1024]{2,1,0:T(8,128)(2,1)} %bitcast.3), channel_id=1, source_target_pairs={{0,4},{4,8},{8,12},{12,16},{16,20},{20,24},{24,28},{28,32},{32,36}... | collective-permute-start | bytes 3145736 | tf_op jit(solution)/shard_map/ppermute | solution.py:18
  13.6 43.7 %collective-permute-start.2 = (bf16[4,128,1024]{2,1,0:T(8,128)(2,1)}, bf16[4,128,1024]{2,1,0:T(8,128)(2,1)}, u32[]{:S(2)}, u32[]{:S(2)}) collective-permute-start(bf16[4,128,1024]{2,1,0:T(8,128)(2,1)} %bitcast.3), channel_id=1, source_target_pairs={{0,252},{4,0},{8,4},{12,8},{16,12},{20,16},{24,20},{28,24},{32,28}... | collective-permute-start | bytes 3145736 | tf_op jit(solution)/shard_map/ppermute | solution.py:18
  19.8 39.8 %collective-permute-start.3 = (bf16[4,128,1024]{2,1,0:T(8,128)(2,1)}, bf16[4,128,1024]{2,1,0:T(8,128)(2,1)}, u32[]{:S(2)}, u32[]{:S(2)}) collective-permute-start(bf16[4,128,1024]{2,1,0:T(8,128)(2,1)} %bitcast.3), channel_id=1, source_target_pairs={{0,248},{4,252},{8,0},{12,4},{16,8},{20,12},{24,16},{28,20},{32,24... | collective-permute-start | bytes 3145736 | tf_op jit(solution)/shard_map/ppermute | solution.py:18
  257.3 4.9 copy-start.1
  259.7 35.9 %collective-permute-start.4 = (bf16[4,128,1024]{2,1,0:T(8,128)(2,1)}, bf16[4,128,1024]{2,1,0:T(8,128)(2,1)}, u32[]{:S(2)}, u32[]{:S(2)}) collective-permute-start(bf16[4,128,1024]{2,1,0:T(8,128)(2,1)} %get-tuple-element.45), channel_id=1, source_target_pairs={{0,248},{4,252},{8,0},{12,4},{16,8},{20,12},{24,16},{28,20},{32,24... | collective-permute-start | bytes 3145736 | tf_op jit(solution)/shard_map/ppermute | solution.py:18
  261.5 34.1 %collective-permute-start.5 = (bf16[4,128,1024]{2,1,0:T(8,128)(2,1)}, bf16[4,128,1024]{2,1,0:T(8,128)(2,1)}, u32[]{:S(2)}, u32[]{:S(2)}) collective-permute-start(bf16[4,128,1024]{2,1,0:T(8,128)(2,1)} %get-tuple-element.48), channel_id=1, source_target_pairs={{0,252},{4,0},{8,4},{12,8},{16,12},{20,16},{24,20},{28,24},{32,28}... | collective-permute-start | bytes 3145736 | tf_op jit(solution)/shard_map/ppermute | solution.py:18
  261.5 34.1 %collective-permute-start.6 = (bf16[4,128,1024]{2,1,0:T(8,128)(2,1)}, bf16[4,128,1024]{2,1,0:T(8,128)(2,1)}, u32[]{:S(2)}, u32[]{:S(2)}) collective-permute-start(bf16[4,128,1024]{2,1,0:T(8,128)(2,1)} %get-tuple-element.47), channel_id=1, source_target_pairs={{0,4},{4,8},{8,12},{12,16},{16,20},{20,24},{24,28},{28,32},{32,36}... | collective-permute-start | bytes 3145736 | tf_op jit(solution)/shard_map/ppermute | solution.py:18
  262.0 33.6 %collective-permute-start.7 = (bf16[4,128,1024]{2,1,0:T(8,128)(2,1)}, bf16[4,128,1024]{2,1,0:T(8,128)(2,1)}, u32[]{:S(2)}, u32[]{:S(2)}) collective-permute-start(bf16[4,128,1024]{2,1,0:T(8,128)(2,1)} %get-tuple-element.46), channel_id=1, source_target_pairs={{0,8},{4,12},{8,16},{12,20},{16,24},{20,28},{24,32},{28,36},{32,40... | collective-permute-start | bytes 3145736 | tf_op jit(solution)/shard_map/ppermute | solution.py:18
  299.4 1.0 copy-start.3
  304.0 2.3 copy-start.4
  575.8 4.0 copy-start.6
Sparse Core Ops, SparseCore 0:
  303.2 272.6 all-reduce.2
where the time goes:
time: 590 us; the launch traced here: 588 us
  waiting for transfers between devices  288 us (49%)
  local copies, waits for them, and re-layouts  118 us (20%)
  matrix products  84.9 us (14%)
  other arithmetic  69.6 us (12%)
  between operations  14.2 us (2%)
  starting transfers between devices  12.7 us (2%)
    psum x1, waiting for transfers between devices, on_device(): lax.psum((local_qkv, local_out), ('patch', 'sample'))  268 us
    scatter-add x1, other arithmetic, advance(): running.at[flat_slots]  36.2 us
    dot_general x1, matrix products, tile_backward(): jnp.einsum('hqk,qhd->khd', dscore, query_heads, preferred_element_type=jn...  24 us
    dot_general x1, matrix products, tile_backward(): jnp.einsum('hqk,khd->qhd', dscore, key_heads, preferred_element_type=jnp....  22.9 us
    concatenate x2, local copies, waits for them, and re-layouts, tile_backward(): return (attended, dquery, jnp.concatenate([dkey, dvalue], -1))  20.6 us
    ppermute x8, waiting for transfers between devices, from_behind(): return lax.ppermute(value, axis, pairs)  20 us
    unnamed x28, local copies, waits for them, and re-layouts  15.8 us
    reshape x2, local copies, waits for them, and re-layouts, tile_backward(): pair_tiles[:, :, :model_width].reshape(-1, head_count, head_width)  14.5 us
  transfers between devices with their start and end apart: 9, of which 3 were waited for; matrix products, arithmetic and copies ran while one was open for 9% of the time, Pallas kernels for 0%

commit v1 on v0

--- a/solution.py
+++ b/solution.py
@@ -139,7 +139,9 @@
     local_out = jnp.einsum(
         "pd,pe->de", attended_rows, grad_rows, preferred_element_type=jnp.float32
     )
-    summed_qkv, summed_out = lax.psum((local_qkv, local_out), ("patch", "sample"))
+    summed_qkv, summed_out = jax.lax.psum(
+        jax.lax.psum((local_qkv, local_out), axis_name="sample"), axis_name="patch"
+    )
     factor = float(lax.axis_size("patch") * lax.axis_size("sample") * rows_local) ** (-0.5)
     return (grad_inputs.astype(jnp.bfloat16)[None], summed_qkv * factor, summed_out * factor)
 

time: 590 us -> 619 us (1.049)
  waiting for transfers between devices: 288 us -> 317 us
    psum x1 -> x2, waiting for transfers between devices: 268 us -> 297 us  [the longest x1 196 us: on_device(): jax.lax.psum(jax.lax.psum((local_qkv, local_out), axis_name='sample'), ax...]
  transfers between devices with their start and end apart: 9 -> 10, of which waited for: 3 -> 4; matrix products, arithmetic and copies ran while one was open for 9% -> 9% of each run, Pallas kernels for 0% -> 0%
where the time goes in v1:
time: 619 us; the launch traced here: 617 us
  waiting for transfers between devices  317 us (51%)
  local copies, waits for them, and re-layouts  118 us (19%)
  matrix products  84.9 us (14%)
  other arithmetic  69.5 us (11%)
  between operations  14.2 us (2%)
  starting transfers between devices  12.7 us (2%)
    psum x1, waiting for transfers between devices, on_device(): jax.lax.psum(jax.lax.psum((local_qkv, local_out), axis_name='sample'), ax...  196 us
    psum x1, waiting for transfers between devices, on_device(): jax.lax.psum((local_qkv, local_out), axis_name='sample')  101 us
    scatter-add x1, other arithmetic, advance(): running.at[flat_slots]  36.1 us
    dot_general x1, matrix products, tile_backward(): jnp.einsum('hqk,qhd->khd', dscore, query_heads, preferred_element_type=jn...  24 us
    dot_general x1, matrix products, tile_backward(): jnp.einsum('hqk,khd->qhd', dscore, key_heads, preferred_element_type=jnp....  22.9 us
    concatenate x2, local copies, waits for them, and re-layouts, tile_backward(): return (attended, dquery, jnp.concatenate([dkey, dvalue], -1))  20.6 us
    ppermute x8, waiting for transfers between devices, from_behind(): return lax.ppermute(value, axis, pairs)  20 us
    unnamed x28, local copies, waits for them, and re-layouts  15.8 us
  transfers between devices with their start and end apart: 10, of which 4 were waited for; matrix products, arithmetic and copies ran while one was open for 9% of the time, Pallas kernels for 0%

profile of v1, /device:TPU:2, one launch (start us, length us, event | category | flops | bytes accessed | tf_op | source)
XLA Modules:
  0.0 616.8 jit_solution(17182172711225214792)
XLA Ops:
  13.6 6.2 %collective-permute-start.2 = (bf16[4,128,1024]{2,1,0:T(8,128)(2,1)}, bf16[4,128,1024]{2,1,0:T(8,128)(2,1)}, u32[]{:S(2)}, u32[]{:S(2)}) collective-permute-start(bf16[4,128,1024]{2,1,0:T(8,128)(2,1)} %bitcast.3), channel_id=1, source_target_pairs={{0,252},{4,0},{8,4},{12,8},{16,12},{20,16},{24,20},{28,24},{32,28}... | collective-permute-start | bytes 3145736 | tf_op jit(solution)/shard_map/ppermute | solution.py:18
  19.8 2.3 collective-permute-start.3
  32.8 11.9 %collective-permute-done = bf16[4,128,1024]{2,1,0:T(8,128)(2,1)} collective-permute-done((bf16[4,128,1024]{2,1,0:T(8,128)(2,1)}, bf16[4,128,1024]{2,1,0:T(8,128)(2,1)}, u32[]{:S(2)}, u32[]{:S(2)}) %collective-permute-start) | collective-permute-done | bytes 1048608 | tf_op jit(solution)/shard_map/ppermute | solution.py:18
  47.0 8.1 %collective-permute-done.1 = bf16[4,128,1024]{2,1,0:T(8,128)(2,1)} collective-permute-done((bf16[4,128,1024]{2,1,0:T(8,128)(2,1)}, bf16[4,128,1024]{2,1,0:T(8,128)(2,1)}, u32[]{:S(2)}, u32[]{:S(2)}) %collective-permute-start.1) | collective-permute-done | bytes 1048608 | tf_op jit(solution)/shard_map/ppermute | solution.py:18
  61.9 7.6 %gather_fusion = bf16[32,128,1024]{2,1,0:T(8,128)(2,1)} fusion(bf16[20,128,1024]{2,1,0:T(8,128)(2,1)} %constant_dynamic-update-slice_fusion, s32[1024]{0:T(1024)S(1)} %pad_clamp_fusion), kind=kCustom, calls=%fused_computation | custom fusion | bytes 16777344 | tf_op jit(solution)/shard_map/while/body/eval_jaxpr/jit(_take)/gather | solution.py:99
  69.5 7.5 %broadcast_select_fusion = bf16[4,8,128,1024]{3,2,1,0:T(8,128)(2,1)} fusion(bf16[4,8,128,1024]{3,2,1,0:T(8,128)(2,1)} %bitcast.63, pred[4,8]{1,0:T(4,128)(4,1)S(1)} %copy.39), kind=kLoop, calls=%fused_computation.10 | loop fusion | flops 4194304 | bytes 16777248 | tf_op jit(solution)/shard_map/while/body/eval_jaxpr/jit(_take)/select_n | solution.py:99
  77.0 5.9 fusion.70
  82.8 6.9 %reshape.155 = bf16[4,1024,4,128]{3,2,1,0:T(4,128)(2,1)} reshape(bf16[4,8,128,512]{3,2,1,0:T(8,128)(2,1)} %get-tuple-element.46) | data formatting | bytes 8388608 | tf_op jit(solution)/shard_map/while/body/eval_jaxpr/vmap()/reshape | solution.py:26
  89.8 7.5 %copy.57 = bf16[4,1024,4,128]{1,3,2,0:T(8,128)(2,1)} copy(bf16[4,1024,4,128]{3,2,1,0:T(4,128)(2,1)} %reshape.155) | data formatting | bytes 8388608 | tf_op jit(solution)/shard_map/while/body/eval_jaxpr/vmap()/reshape | solution.py:26
  97.3 6.9 %reshape.156 = bf16[4,1024,4,128]{3,2,1,0:T(4,128)(2,1)} reshape(bf16[4,8,128,512]{3,2,1,0:T(8,128)(2,1)} %get-tuple-element.45) | data formatting | bytes 8388608 | tf_op jit(solution)/shard_map/while/body/eval_jaxpr/vmap()/reshape | solution.py:27
  104.2 7.5 %copy.56 = bf16[4,1024,4,128]{1,3,2,0:T(8,128)(2,1)} copy(bf16[4,1024,4,128]{3,2,1,0:T(4,128)(2,1)} %reshape.156) | data formatting | bytes 8388608 | tf_op jit(solution)/shard_map/while/body/eval_jaxpr/vmap()/reshape | solution.py:27
  111.7 6.7 %fusion.73 = f32[4,4,128,1024]{3,2,1,0:T(8,128)} fusion(bf16[4,128,4,128]{1,3,2,0:T(8,128)(2,1)S(1)} %copy.51, bf16[4,1024,4,128]{1,3,2,0:T(8,128)(2,1)} %copy.56), kind=kOutput, calls=%fused_computation.98 | convolution fusion | flops 536870912 | bytes 13107200 | tf_op jit(solution)/shard_map/while/body/eval_jaxpr/vmap(qhd,khd->hqk)/dot_general | solution.py:44
  118.4 8.8 %fusion.72 = (f32[4,4,128]{2,1,0:T(4,128)S(1)}, f32[4,4,128,1024]{3,2,1,0:T(8,128)}) fusion(pred[4,1024]{1,0:T(4,128)(4,1)S(1)} %bitcast.70, bf16[4,128,4,128]{1,3,2,0:T(8,128)(2,1)} %copy.49, bf16[4,1024,4,128]{1,3,2,0:T(8,128)(2,1)} %copy.57), kind=kOutput, calls=%fused_computation.97 | convolution fusion | flops 545260544 | bytes 13119488 | tf_op jit(solution)/shard_map/while/body/eval_jaxpr/vmap()/sub | solution.py:37
  127.2 8.0 %convolution_bitcast_fusion = f32[4,1024,4,128]{1,3,2,0:T(8,128)} fusion(bf16[4,128,4,128]{1,3,2,0:T(8,128)(2,1)S(1)} %copy.51, f32[4,4,128,1024]{3,2,1,0:T(8,128)} %get-tuple-element.52, f32[4,4,128]{2,1,0:T(4,128)S(1)} %get-tuple-element.51), kind=kOutput, calls=%fused_computation.19 | convolution fusion | flops 541065216 | bytes 17309696 | tf_op jit(solution)/shard_map/while/body/eval_jaxpr/vmap(hqk,qhd->khd)/dot_general | solution.py:51
  135.1 24.0 %fusion.15 = f32[4,1024,4,128]{1,3,2,0:T(8,128)} fusion(bf16[4,128,4,128]{1,3,2,0:T(8,128)(2,1)} %copy.49, f32[4,4,128,1024]{3,2,1,0:T(8,128)} %fusion.73, f32[4,4,128,1024]{3,2,1,0:T(8,128)} %get-tuple-element.52, f32[4,4,128]{2,1,0:T(4,128)S(1)} %get-tuple-element.51), kind=kOutput, calls=%fused_computation.18 | convolution fusion | flops 551554048 | bytes 25698304 | tf_op jit(solution)/shard_map/while/body/eval_jaxpr/vmap(hqk,qhd->khd)/dot_general | solution.py:50
  159.1 9.9 %copy.50 = f32[4,1024,4,128]{3,2,1,0:T(4,128)} copy(f32[4,1024,4,128]{1,3,2,0:T(8,128)} %fusion.15) | data formatting | bytes 16777216 | tf_op jit(solution)/shard_map/while/body/eval_jaxpr/vmap(hqk,qhd->khd)/transpose | solution.py:50
  169.0 10.3 %concatenate.17 = f32[32,128,512]{2,1,0:T(8,128)} reshape(f32[4,1024,4,128]{3,2,1,0:T(4,128)} %copy.50) | data formatting | bytes 16777216 | tf_op jit(solution)/shard_map/while/body/eval_jaxpr/vmap()/concatenate | solution.py:56
  179.3 9.9 %copy.52 = f32[4,1024,4,128]{3,2,1,0:T(4,128)} copy(f32[4,1024,4,128]{1,3,2,0:T(8,128)} %convolution_bitcast_fusion) | data formatting | bytes 16777216 | tf_op jit(solution)/shard_map/while/body/eval_jaxpr/vmap(hqk,qhd->khd)/transpose | solution.py:51
  189.1 10.3 %concatenate.18 = f32[32,128,512]{2,1,0:T(8,128)} reshape(f32[4,1024,4,128]{3,2,1,0:T(4,128)} %copy.52) | data formatting | bytes 16777216 | tf_op jit(solution)/shard_map/while/body/eval_jaxpr/vmap()/concatenate | solution.py:56
  199.4 11.7 %pad_maximum_fusion = f32[32,128,1024]{2,1,0:T(8,128)} fusion(f32[32,128,512]{2,1,0:T(8,128)} %concatenate.18, f32[32,128,512]{2,1,0:T(8,128)} %concatenate.17), kind=kLoop, calls=%fused_computation.4 | loop fusion | flops 4194304 | bytes 33554432 | tf_op jit(solution)/shard_map/while/body/eval_jaxpr/vmap()/concatenate | solution.py:56
  211.1 5.2 broadcast_in_dim.64
  216.3 36.1 %scatter_fusion = f32[20,128,1024]{2,1,0:T(8,128)} fusion(f32[20,128,1024]{2,1,0:T(8,128)} %broadcast_in_dim.64, s32[32]{0:T(128)S(1)} %fusion.61, f32[32,128,1024]{2,1,0:T(8,128)} %pad_maximum_fusion), kind=kCustom, calls=%fused_computation.1 | custom fusion | flops 4194304 | bytes 50331776 | tf_op jit(solution)/shard_map/while/body/eval_jaxpr/scatter-add | solution.py:103
  252.5 4.8 convert.17
  257.3 2.3 fusion.71
  262.2 4.7 fusion.34
  268.0 22.9 %fusion.37 = bf16[4,128,4,128]{1,3,2,0:T(8,128)(2,1)S(1)} fusion(bf16[4,1024,4,128]{1,3,2,0:T(8,128)(2,1)} %copy.57, f32[4,4,128,1024]{3,2,1,0:T(8,128)} %fusion.73, f32[4,4,128,1024]{3,2,1,0:T(8,128)} %get-tuple-element.52, f32[4,4,128]{2,1,0:T(4,128)S(1)} %get-tuple-element.51), kind=kOutput, calls=%fused_computation.40 | convolution fusion | flops 551816192 | bytes 21504000 | tf_op jit(solution)/shard_map/while/body/eval_jaxpr/vmap(hqk,khd->qhd)/dot_general | solution.py:47
  293.1 2.5 fusion.49
  295.6 3.8 fusion.21
  300.4 2.7 fusion.46
  303.1 100.7 %all-reduce.7.cloned.1.call-done = (f32[512,1536]{1,0:T(8,128)}, f32[512,512]{1,0:T(8,128)}) async-done(((f32[512,1536]{1,0:T(8,128)}, f32[512,512]{1,0:T(8,128)}), (f32[512,1536]{1,0:T(8,128)}, f32[512,512]{1,0:T(8,128)})) %all-reduce.7.cloned.1.call-update) | async-done | bytes 4194320 | tf_op jit(solution)/shard_map/psum | solution.py:143
  408.5 196.5 %all-reduce.5.cloned.1.call-done = (f32[512,1536]{1,0:T(8,128)}, f32[512,512]{1,0:T(8,128)}) async-done(((f32[512,1536]{1,0:T(8,128)}, f32[512,512]{1,0:T(8,128)}), (f32[512,1536]{1,0:T(8,128)}, f32[512,512]{1,0:T(8,128)})) %all-reduce.5.cloned.1.call-update) | async-done | bytes 4194320 | tf_op jit(solution)/shard_map/psum | solution.py:142
  605.0 4.0 broadcast_multiply_fusion
  (68 shorter events, 38.7 us)
Async XLA Ops:
  7.2 1.6 copy-start
  7.2 15.0 %copy-start.7 = (s32[256,8]{0,1:T(8,128)S(1)}, s32[256,8]{0,1:T(8,128)}, u32[]{:S(2)}) copy-start(s32[256,8]{0,1:T(8,128)} %param.10) | copy-start | bytes 24580
  7.2 15.0 %copy-start.8 = (s32[256,8]{0,1:T(8,128)S(1)}, s32[256,8]{0,1:T(8,128)}, u32[]{:S(2)}) copy-start(s32[256,8]{0,1:T(8,128)} %param.11) | copy-start | bytes 24580
  7.2 396.6 %all-reduce.7.cloned.1.call-start = ((), (), s32[]{:S(2)}) async-start(), calls=%async_computation.1 | async-start | bytes 8388608 | tf_op jit(solution)/shard_map/psum | solution.py:143
  8.8 18.0 %copy-start.2 = (bf16[1,512,512]{2,1,0:T(8,128)(2,1)S(1)}, bf16[1,512,512]{2,1,0:T(8,128)(2,1)}, u32[]{:S(2)}) copy-start(bf16[1,512,512]{2,1,0:T(8,128)(2,1)} %param.7) | copy-start | bytes 1572868
  9.8 1.1 copy-start.5
  12.1 32.6 %collective-permute-start = (bf16[4,128,1024]{2,1,0:T(8,128)(2,1)}, bf16[4,128,1024]{2,1,0:T(8,128)(2,1)}, u32[]{:S(2)}, u32[]{:S(2)}) collective-permute-start(bf16[4,128,1024]{2,1,0:T(8,128)(2,1)} %bitcast.3), channel_id=1, source_target_pairs={{0,8},{4,12},{8,16},{12,20},{16,24},{20,28},{24,32},{28,36},{32,40... | collective-permute-start | bytes 3145736 | tf_op jit(solution)/shard_map/ppermute | solution.py:18
  13.6 41.4 %collective-permute-start.1 = (bf16[4,128,1024]{2,1,0:T(8,128)(2,1)}, bf16[4,128,1024]{2,1,0:T(8,128)(2,1)}, u32[]{:S(2)}, u32[]{:S(2)}) collective-permute-start(bf16[4,128,1024]{2,1,0:T(8,128)(2,1)} %bitcast.3), channel_id=1, source_target_pairs={{0,4},{4,8},{8,12},{12,16},{16,20},{20,24},{24,28},{28,32},{32,36}... | collective-permute-start | bytes 3145736 | tf_op jit(solution)/shard_map/ppermute | solution.py:18
  13.6 43.7 %collective-permute-start.2 = (bf16[4,128,1024]{2,1,0:T(8,128)(2,1)}, bf16[4,128,1024]{2,1,0:T(8,128)(2,1)}, u32[]{:S(2)}, u32[]{:S(2)}) collective-permute-start(bf16[4,128,1024]{2,1,0:T(8,128)(2,1)} %bitcast.3), channel_id=1, source_target_pairs={{0,252},{4,0},{8,4},{12,8},{16,12},{20,16},{24,20},{28,24},{32,28}... | collective-permute-start | bytes 3145736 | tf_op jit(solution)/shard_map/ppermute | solution.py:18
  19.8 39.8 %collective-permute-start.3 = (bf16[4,128,1024]{2,1,0:T(8,128)(2,1)}, bf16[4,128,1024]{2,1,0:T(8,128)(2,1)}, u32[]{:S(2)}, u32[]{:S(2)}) collective-permute-start(bf16[4,128,1024]{2,1,0:T(8,128)(2,1)} %bitcast.3), channel_id=1, source_target_pairs={{0,248},{4,252},{8,0},{12,4},{16,8},{20,12},{24,16},{28,20},{32,24... | collective-permute-start | bytes 3145736 | tf_op jit(solution)/shard_map/ppermute | solution.py:18
  257.3 4.9 copy-start.1
  259.6 35.9 %collective-permute-start.4 = (bf16[4,128,1024]{2,1,0:T(8,128)(2,1)}, bf16[4,128,1024]{2,1,0:T(8,128)(2,1)}, u32[]{:S(2)}, u32[]{:S(2)}) collective-permute-start(bf16[4,128,1024]{2,1,0:T(8,128)(2,1)} %get-tuple-element.47), channel_id=1, source_target_pairs={{0,248},{4,252},{8,0},{12,4},{16,8},{20,12},{24,16},{28,20},{32,24... | collective-permute-start | bytes 3145736 | tf_op jit(solution)/shard_map/ppermute | solution.py:18
  261.5 34.0 %collective-permute-start.5 = (bf16[4,128,1024]{2,1,0:T(8,128)(2,1)}, bf16[4,128,1024]{2,1,0:T(8,128)(2,1)}, u32[]{:S(2)}, u32[]{:S(2)}) collective-permute-start(bf16[4,128,1024]{2,1,0:T(8,128)(2,1)} %get-tuple-element.50), channel_id=1, source_target_pairs={{0,252},{4,0},{8,4},{12,8},{16,12},{20,16},{24,20},{28,24},{32,28}... | collective-permute-start | bytes 3145736 | tf_op jit(solution)/shard_map/ppermute | solution.py:18
  261.5 34.0 %collective-permute-start.6 = (bf16[4,128,1024]{2,1,0:T(8,128)(2,1)}, bf16[4,128,1024]{2,1,0:T(8,128)(2,1)}, u32[]{:S(2)}, u32[]{:S(2)}) collective-permute-start(bf16[4,128,1024]{2,1,0:T(8,128)(2,1)} %get-tuple-element.49), channel_id=1, source_target_pairs={{0,4},{4,8},{8,12},{12,16},{16,20},{20,24},{24,28},{28,32},{32,36}... | collective-permute-start | bytes 3145736 | tf_op jit(solution)/shard_map/ppermute | solution.py:18
  262.0 33.5 %collective-permute-start.7 = (bf16[4,128,1024]{2,1,0:T(8,128)(2,1)}, bf16[4,128,1024]{2,1,0:T(8,128)(2,1)}, u32[]{:S(2)}, u32[]{:S(2)}) collective-permute-start(bf16[4,128,1024]{2,1,0:T(8,128)(2,1)} %get-tuple-element.48), channel_id=1, source_target_pairs={{0,8},{4,12},{8,16},{12,20},{16,24},{20,28},{24,32},{28,36},{32,40... | collective-permute-start | bytes 3145736 | tf_op jit(solution)/shard_map/ppermute | solution.py:18
  299.4 1.0 copy-start.3
  303.0 301.9 %all-reduce.5.cloned.1.call-start = ((), (), s32[]{:S(2)}) async-start(), calls=%async_computation | async-start | bytes 8388608 | tf_op jit(solution)/shard_map/psum | solution.py:142
  404.9 2.3 copy-start.4
  605.0 4.0 copy-start.6
Sparse Core Ops, SparseCore 0:
  303.2 100.6 all-reduce.6
  407.9 197.0 all-reduce.4
